TPU v7x, 32 devices: a whole 2x2x4 slice. The times are simulated.
32 devices in a mesh: gy: 8 (over y, x, core), pa: 4 (over z).
Axes of the slice: x: 2, y: 2, z: 4, core: 2. Of those that a mesh axis runs over, the one named last changes fastest.
Arguments:
- spectral_velocity: float32 [3, 16, 512, 1536], P(None, 'gy', 'pa'), may hold values from -0.01913664 to 0.01913664
- inverse_spacing: float32 [16], P('gy'), may hold values from 0.25 to 1
Outputs:
- increment: float32 [3, 16, 1152, 1536], P(None, 'gy', 'pa')
- vorticity_peak: float32 [], replicated
All inputs are finite; a program needn't handle non-finite values.
Results may differ from a plain program's by a relative error of at most 0.00011.
Values sent between devices are 32-bit elements; how exact they have to be, the bound alone decides.
A program may use at most 128 MiB of HBM per device.

v0:
```python
from functools import partial
import math

import jax
import jax.numpy as jnp
from jax import lax
from jax.sharding import PartitionSpec as P

NX = 1536
NZ = 1152
KX = 512


def with_halo(cells, sides, width):
    for axis, dim in sides:
        count = lax.axis_size(axis)
        ends = count - 1
        head = lax.slice_in_dim(cells, 0, width, axis=dim)
        tail = lax.slice_in_dim(cells, cells.shape[dim] - width, cells.shape[dim], axis=dim)
        cells = jnp.concatenate(
            [
                lax.ppermute(tail, axis, [(i, (i + 1) % count) for i in range(ends)]),
                cells,
                lax.ppermute(head, axis, [((i + 1) % count, i) for i in range(ends)]),
            ],
            axis=dim,
        )
    return cells


def z_tables(length, modes):
    column = jnp.arange(modes, dtype=jnp.int32)
    wave = jnp.where(column < modes // 2, column, column - modes)
    points = jnp.arange(length, dtype=jnp.int32)
    phase = wave[:, None] * points[None, :] % length
    angles = phase.astype(jnp.float32) * (2.0 * math.pi / length)
    return (jnp.cos(angles), jnp.sin(angles))


def x_tables(length, modes):
    column = jnp.arange(modes, dtype=jnp.int32)
    points = jnp.arange(length, dtype=jnp.int32)
    phase = column[:, None] * points[None, :] % length
    angles = phase.astype(jnp.float32) * (2.0 * math.pi / length)
    weight = jnp.where(column == 0, 1.0, 2.0).astype(jnp.float32)[:, None]
    return (weight * jnp.cos(angles), -weight * jnp.sin(angles))


def to_z(real_part, imag_part, cos_z, sin_z):
    product = partial(jnp.dot, precision=lax.Precision.HIGHEST, preferred_element_type=jnp.float32)
    real_out = product(real_part, cos_z) - product(imag_part, sin_z)
    imag_out = product(real_part, sin_z) + product(imag_part, cos_z)
    return jnp.stack((real_out, imag_out), axis=-2)


def to_x(received, cos_x, sin_x):
    first = jnp.einsum(
        "fkmz,mx->fkzx", received[:, :, :, 0], cos_x, precision=lax.Precision.HIGHEST
    )
    second = jnp.einsum(
        "fkmz,mx->fkzx", received[:, :, :, 1], sin_x, precision=lax.Precision.HIGHEST
    )
    return first + second


def times_wave(real_part, imag_part, wave):
    return (-wave * imag_part, wave * real_part)


def body(spectral_velocity, inverse_spacing):
    modes_z = spectral_velocity.shape[3] // 2
    kx_local = spectral_velocity.shape[2]
    cos_z, sin_z = z_tables(NZ, modes_z)
    cos_x, sin_x = x_tables(NX, KX)
    first_mode = lax.axis_index("pa") * kx_local
    wave_x = (
        (first_mode + jnp.arange(kx_local, dtype=jnp.int32)).astype(jnp.float32)
        * (2.0 * math.pi / NX)
    )[:, None]
    column = jnp.arange(modes_z, dtype=jnp.int32)
    wave_z = jnp.where(column < modes_z // 2, column, column - modes_z).astype(jnp.float32) * (
        2.0 * math.pi / NZ
    )
    real_part = spectral_velocity[..., :modes_z]
    imag_part = spectral_velocity[..., modes_z:]
    transform_x = partial(to_x, cos_x=cos_x, sin_x=sin_x)
    spacing = inverse_spacing[:, None, None]
    dz_v = times_wave(real_part[1], imag_part[1], wave_z)
    dz_u = times_wave(real_part[0], imag_part[0], wave_z)
    dx_w = times_wave(real_part[2], imag_part[2], wave_x)
    dx_v = times_wave(real_part[1], imag_part[1], wave_x)
    real_all = jnp.concatenate((real_part, jnp.stack((dz_v[0], dz_u[0] - dx_w[0], dx_v[0]))), 0)
    imag_all = jnp.concatenate((imag_part, jnp.stack((dz_v[1], dz_u[1] - dx_w[1], dx_v[1]))), 0)
    spectra = to_z(real_all, imag_all, cos_z, sin_z)
    fields = transform_x(lax.all_to_all(spectra, "pa", split_axis=4, concat_axis=2, tiled=True))
    pair_phys = jnp.stack((fields[0], fields[2]))
    extended = with_halo(pair_phys, (("gy", 1),), 1)
    normal_diff = (extended[:, 2:] - extended[:, :-2]) * spacing
    vort_x = normal_diff[1] - fields[3]
    vort_z = fields[5] - normal_diff[0]
    vort_y = fields[4]
    lamb = jnp.stack(
        (
            fields[1] * vort_z - fields[2] * vort_y,
            fields[2] * vort_x - fields[0] * vort_z,
            fields[0] * vort_y - fields[1] * vort_x,
        )
    )
    local_peak = jnp.max(vort_x * vort_x + vort_y * vort_y + vort_z * vort_z)
    peak_square = lax.pmax(local_peak, ("gy", "pa"))
    magnitude = jnp.sqrt(peak_square)
    return (lamb / (magnitude + 1e-06), magnitude)


def solution(mesh):
    placed = (P(None, "gy", "pa", None), P("gy"))
    return jax.shard_map(
        body,
        mesh=mesh,
        in_specs=placed,
        out_specs=(P(None, "gy", "pa", None), P()),
        check_vma=False,
    )
```

profile of v0, /device:TPU:0, one launch (start us, length us, event | category | flops | bytes accessed | tf_op | source)
XLA Modules:
  0.0 887.9 jit_solution(57470587156587398)
XLA Ops:
  0.7 2.8 fusion.85
  3.5 0.9 copy-done.2
  4.4 0.5 slice_multiply_fusion.1
  4.9 0.3 pad_maximum_fusion.24
  6.2 55.2 %fusion.7 = f32[6,2,128,1152]{3,2,1,0:T(8,128)} fusion(s32[768]{0:T(1024)S(1)} %compare_select_fusion, f32[6,2,128,768]{3,2,1,0:T(8,128)S(1)} %pad_maximum_fusion.26), kind=kOutput, calls=%fused_computation.27 | convolution fusion | flops 16315416576 | bytes 11799552 | tf_op jit(solution)/shard_map/dot_general | solution.py:51
  61.4 37.7 %fusion.9 = f32[6,2,128,1152]{3,2,1,0:T(8,128)S(1)} fusion(s32[768]{0:T(1024)S(1)} %compare_select_fusion, f32[6,2,128,768]{3,2,1,0:T(8,128)S(1)} %pad_maximum_fusion.27), kind=kOutput, calls=%fused_computation.29 | convolution fusion | flops 16315416576 | bytes 11799552 | tf_op jit(solution)/shard_map/dot_general | solution.py:52
  99.0 40.0 %subtract_bitcast_fusion = f32[6,2,128,1,1152]{4,2,1,0,3:T(8,128)} fusion(f32[6,2,128,1152]{3,2,1,0:T(8,128)} %fusion.7, s32[768]{0:T(1024)S(1)} %compare_select_fusion, f32[6,2,128,768]{3,2,1,0:T(8,128)S(1)} %pad_maximum_fusion.25), kind=kOutput, calls=%fused_computation.15 | convolution fusion | flops 16317186048 | bytes 18877440 | tf_op jit(solution)/shard_map/dot_general | solution.py:51
  139.0 77.1 %add_bitcast_fusion = f32[6,2,128,1,1152]{4,2,1,0,3:T(8,128)} fusion(f32[6,2,128,1152]{3,2,1,0:T(8,128)S(1)} %fusion.9, s32[768]{0:T(1024)S(1)} %compare_select_fusion, f32[6,2,128,768]{3,2,1,0:T(8,128)S(1)} %pad_maximum_fusion.24), kind=kOutput, calls=%fused_computation.14 | convolution fusion | flops 16317186048 | bytes 18877440 | tf_op jit(solution)/shard_map/dot_general | solution.py:52
  216.1 11.4 %pad_maximum_fusion = f32[6,2,128,2,1152]{4,2,1,0,3:T(8,128)} fusion(f32[6,2,128,1,1152]{4,2,1,0,3:T(8,128)} %add_bitcast_fusion, f32[6,2,128,1,1152]{4,2,1,0,3:T(8,128)} %subtract_bitcast_fusion), kind=kLoop, calls=%fused_computation.1 | loop fusion | flops 3538944 | bytes 28311552 | tf_op jit(solution)/shard_map/stack | solution.py:53
  227.5 21.7 %copy.7 = f32[6,2,128,2,1152]{2,1,0,3,4:T(2,128)} copy(f32[6,2,128,2,1152]{4,2,1,0,3:T(8,128)} %pad_maximum_fusion) | data formatting | bytes 28311552 | tf_op jit(solution)/shard_map/stack | solution.py:53
  249.2 6.6 all-to-all-start
  255.8 308.4 %all-to-all-done = f32[6,2,128,2,1152]{2,1,0,3,4:T(2,128)} async-done(((f32[6,2,128,2,1152]{2,1,0,3,4:T(2,128)}), f32[6,2,128,2,1152]{2,1,0,3,4:T(2,128)}, u32[]{:S(2)}, u32[]{:S(2)}) %all-to-all-start) | async-done | bytes 14155808 | tf_op jit(solution)/shard_map/all_to_all | solution.py:95
  564.2 12.9 %copy.8 = f32[6,2,128,2,1152]{2,4,3,1,0:T(8,128)} copy(f32[6,2,128,2,1152]{2,1,0,3,4:T(2,128)} %all-to-all-done) | data formatting | bytes 28311552 | tf_op jit(solution)/shard_map/all_to_all | solution.py:95
  577.1 17.6 %copy.9 = f32[6,2,4,128,2,288]{3,2,5,1,0,4:T(4,128)} copy(f32[6,2,4,128,2,288]{3,5,2,4,1,0:T(8,128)} %bitcast.75) | data formatting | bytes 28311552 | tf_op jit(solution)/shard_map/all_to_all | solution.py:95
  594.6 17.3 %all_to_all.16 = f32[6,2,512,2,288]{2,4,1,0,3:T(8,128)} reshape(f32[6,2,4,128,2,288]{3,2,5,1,0,4:T(4,128)} %copy.9) | data formatting | bytes 28311552 | tf_op jit(solution)/shard_map/all_to_all | solution.py:95
  612.0 7.6 slice_bitcast_fusion.10
  619.6 2.0 copy-done.1
  621.6 0.8 slice_bitcast_fusion.11
  622.4 50.6 %fusion.2 = f32[6,2,288,1536]{3,2,1,0:T(8,128)} fusion(f32[512]{0:T(512)S(1)} %fusion.58, f32[6,2,512,288]{2,3,1,0:T(8,128)S(1)} %slice_bitcast_fusion.11), kind=kOutput, calls=%fused_computation.11 | convolution fusion | flops 32622772224 | bytes 28313600 | tf_op jit(solution)/shard_map/fkmz,mx->fkzx/dot_general | solution.py:57
  673.0 52.1 %convolution_add_fusion = f32[6,2,288,1536]{3,2,1,0:T(8,128)S(1)} fusion(f32[6,2,288,1536]{3,2,1,0:T(8,128)} %fusion.2, f32[512]{0:T(512)S(1)} %fusion.60, f32[6,2,512,288]{2,3,1,0:T(8,128)} %slice_bitcast_fusion.10), kind=kOutput, calls=%fused_computation | convolution fusion | flops 32628080640 | bytes 49547264 | tf_op jit(solution)/shard_map/fkmz,mx->fkzx/dot_general | solution.py:60
  725.1 2.7 fusion.84
  727.9 8.2 fusion.5
  736.0 0.8 copy-done
  736.8 1.3 collective-permute-start
  738.1 3.3 collective-permute-start.1
  741.4 3.8 collective-permute-done
  745.1 2.1 collective-permute-done.1
  747.2 3.3 fusion.1
  750.5 9.0 %multiply_subtract_fusion.2 = f32[1,2,288,1536]{3,2,1,0:T(8,128)} fusion(f32[6,2,288,1536]{3,2,1,0:T(8,128)} %copy-done, f32[2,2,288,1536]{3,2,1,0:T(8,128)S(1)} %fusion.1), kind=kLoop, calls=%fused_computation.35 | loop fusion | flops 3538944 | bytes 21233664 | tf_op jit(solution)/shard_map/sub | solution.py:104
  759.6 10.8 %add_reduce_fusion = (f32[]{:T(128)}, f32[1,2,288,1536]{3,2,1,0:T(8,128)S(1)}, f32[1,2,288,1536]{3,2,1,0:T(8,128)}) fusion(f32[6,2,288,1536]{3,2,1,0:T(8,128)} %copy-done, f32[2,2,288,1536]{3,2,1,0:T(8,128)S(1)} %fusion.1), kind=kLoop, calls=%fused_computation.32 | loop fusion | flops 12386303 | bytes 35389444 | tf_op jit(solution)/shard_map/reduce_max | solution.py:109
  770.4 107.8 %pmax.7 = f32[]{:T(128)} all-reduce(f32[]{:T(128)} %get-tuple-element.2), channel_id=1, replica_groups=mesh['gy'=8,'pa'=4] {'gy','pa'}, use_global_device_ids=true, to_apply=%region_1.2 | all-reduce | flops 1 | bytes 8 | tf_op jit(solution)/shard_map/pmax | solution.py:110
  878.9 7.7 maximum_divide_fusion
  (13 shorter events, 1.0 us)
Async XLA Ops:
  0.7 3.8 copy-start.2
  249.2 315.0 %all-to-all-start = ((f32[6,2,128,2,1152]{2,1,0,3,4:T(2,128)}), f32[6,2,128,2,1152]{2,1,0,3,4:T(2,128)}, u32[]{:S(2)}, u32[]{:S(2)}) async-start(f32[6,2,128,2,1152]{2,1,0,3,4:T(2,128)} %copy.7), calls=%async_computation | async-start | bytes 28311552 | tf_op jit(solution)/shard_map/all_to_all | solution.py:95
  612.0 9.6 %copy-start.1 = (f32[6,2,512,2,288]{2,4,1,0,3:T(8,128)S(1)}, f32[6,2,512,2,288]{2,4,1,0,3:T(8,128)}, u32[]{:S(2)}) copy-start(f32[6,2,512,2,288]{2,4,1,0,3:T(8,128)} %all_to_all.16) | copy-start | bytes 42467332
  725.1 11.7 %copy-start = (f32[6,2,288,1536]{3,2,1,0:T(8,128)}, f32[6,2,288,1536]{3,2,1,0:T(8,128)S(1)}, u32[]{:S(2)}) copy-start(f32[6,2,288,1536]{3,2,1,0:T(8,128)S(1)} %convolution_add_fusion) | copy-start | bytes 63700996
  727.9 19.3 %copy-start.3 = (f32[2]{0:T(128)S(1)}, f32[2]{0:T(128)}, u32[]{:S(2)}) copy-start(f32[2]{0:T(128)} %param.3) | copy-start | bytes 28
  736.8 8.3 collective-permute-start
  738.1 9.1 %collective-permute-start.1 = (f32[2,1,288,1536]{3,2,1,0:T(8,128)}, f32[2,1,288,1536]{3,2,1,0:T(8,128)S(1)}, u32[]{:S(2)}, u32[]{:S(2)}) collective-permute-start(f32[2,1,288,1536]{3,2,1,0:T(8,128)} %get-tuple-element.8), channel_id=1, source_target_pairs={{0,4},{4,8},{8,12},{12,16},{16,20},{20,24},{24,28},{1,5},{5,9},{9,... | collective-permute-start | bytes 10616840 | tf_op jit(solution)/shard_map/ppermute | solution.py:22
where the time goes:
time: 894 us; the launch traced here: 888 us
  waiting for transfers between devices  314 us (35%)
  matrix products  313 us (35%)
  blocking collectives  108 us (12%)
  local copies, waits for them, and re-layouts  87.1 us (10%)
  other arithmetic  52.2 us (6%)
  starting transfers between devices  11.1 us (1%)
    all_to_all x1, waiting for transfers between devices, body(): lax.all_to_all(spectra, 'pa', split_axis=4, concat_axis=2, tiled=True)  308 us
    dot_general x2, matrix products, to_z(): imag_out = product(real_part, sin_z) + product(imag_part, cos_z)  115 us
    pmax x1, blocking collectives, body(): peak_square = lax.pmax(local_peak, ('gy', 'pa'))  108 us
    dot_general x2, matrix products, to_z(): real_out = product(real_part, cos_z) - product(imag_part, sin_z)  95.1 us
    dot_general x1, matrix products, to_x(): jnp.einsum('fkmz,mx->fkzx', received[:, :, :, 1], sin_x, precision=lax.Pr...  52.1 us
    dot_general x1, matrix products, to_x(): jnp.einsum('fkmz,mx->fkzx', received[:, :, :, 0], cos_x, precision=lax.Pr...  50.6 us
    all_to_all x3, local copies, waits for them, and re-layouts, body(): lax.all_to_all(spectra, 'pa', split_axis=4, concat_axis=2, tiled=True)  47.8 us
    another operation x1, local copies, waits for them, and re-layouts, to_z(): return jnp.stack((real_out, imag_out), axis=-2)  21.7 us
  transfers between devices with their start and end apart: 3, of which 3 were waited for; matrix products, arithmetic and copies ran while one was open for 0% of the time, Pallas kernels for 0%

commit v1 on v0

v1 whole, which is shorter than its diff:
```python
import math

import numpy as np

import jax
import jax.numpy as jnp
from jax import lax
from jax.sharding import PartitionSpec as P

NX = 1536
NZ = 1152
KX = 512


def z_table(length, modes, parts):
    column = np.arange(modes)
    wave = np.where(column < modes // 2, column, column - modes)
    angles = (wave[None, :] * np.arange(length)[:, None] % length) * (2.0 * math.pi / length)
    cos, sin = np.cos(angles), np.sin(angles)
    scale = (wave * (2.0 * math.pi / length))[None, :]

    def lay(rr, ri, ir, ii):
        real = np.concatenate((rr, ri), 1).reshape(parts, 1, length // parts, 2 * modes)
        imag = np.concatenate((ir, ii), 1).reshape(parts, 1, length // parts, 2 * modes)
        both = np.concatenate((real, imag), 1)
        return both.reshape(parts, -1, 2 * modes).astype(np.float32)

    plain = lay(cos, -sin, sin, cos)
    slope = lay(-scale * sin, -scale * cos, scale * cos, -scale * sin)
    return plain, slope


def x_table(length, modes, parts):
    column = np.arange(modes)
    angles = (column[:, None] * np.arange(length)[None, :] % length) * (2.0 * math.pi / length)
    weight = np.where(column == 0, 1.0, 2.0)[:, None]
    both = np.stack((weight * np.cos(angles), -weight * np.sin(angles)))
    both = both.reshape(2, parts, modes // parts, length)
    return np.moveaxis(both, 1, 0).astype(np.float32)


def everywhere_max(value, axes):
    for axis in axes:
        count = lax.axis_size(axis)
        shift = 1
        while shift < count:
            pairs = [(i, (i + shift) % count) for i in range(count)]
            value = jnp.maximum(value, lax.ppermute(value, axis, pairs))
            shift *= 2
    return value


def body(spectral_velocity, inverse_spacing):
    planes, kx_local, width = spectral_velocity.shape[1:]
    parts = lax.axis_size("pa")
    levels = lax.axis_size("gy")
    me = lax.axis_index("pa")
    slab = NZ // parts
    plain, slope = z_table(NZ, width // 2, parts)
    order = (me - jnp.arange(parts)) % parts
    pieces = x_table(NX, KX, parts)
    pieces = np.concatenate([pieces[[-k % parts]] for k in range(2 * parts)])
    pieces = np.ascontiguousarray(np.moveaxis(pieces, 1, 0)).reshape(2, -1, NX)
    table_x = lax.dynamic_slice_in_dim(
        jnp.asarray(pieces), (parts - me) * kx_local, KX, axis=1
    ).reshape(2 * KX, NX)
    kx = (order[:, None] * kx_local + jnp.arange(kx_local)[None, :]).reshape(-1)
    wave_x = kx.astype(jnp.float32) * (2.0 * math.pi / NX)

    def exchange(modes, table):
        out = jnp.einsum(
            "dnk,fjmk->dfjnm", table, modes, precision=lax.Precision.HIGH,
            preferred_element_type=jnp.float32,
        )
        got = [lax.dynamic_index_in_dim(out, me, 0, keepdims=False)]
        for shift in range(1, parts):
            block = lax.dynamic_index_in_dim(out, (me + shift) % parts, 0, keepdims=False)
            got.append(lax.ppermute(block, "pa", [(i, (i + shift) % parts) for i in range(parts)]))
        whole = jnp.concatenate(got, axis=-1)
        return whole.reshape(whole.shape[:2] + (2, slab, KX))

    def to_x(hat):
        flat = jnp.concatenate((hat[..., 0, :, :], hat[..., 1, :, :]), axis=-1)
        return jnp.einsum(
            "...zm,mx->...zx", flat, table_x, precision=lax.Precision.HIGH,
            preferred_element_type=jnp.float32,
        )

    def turned(hat):
        return jnp.stack((-wave_x * hat[..., 1, :, :], wave_x * hat[..., 0, :, :]), axis=-3)

    u_modes, v_modes, w_modes = (spectral_velocity[c : c + 1] for c in range(3))
    uw_hat = exchange(jnp.concatenate((u_modes, w_modes)), plain)
    dzu_hat = exchange(u_modes, slope)[0]
    v_hat = exchange(v_modes, plain)[0]
    dzv_hat = exchange(v_modes, slope)[0]

    below = lax.ppermute(uw_hat[:, -1:], "gy", [(i, i + 1) for i in range(levels - 1)])
    above = lax.ppermute(uw_hat[:, :1], "gy", [(i + 1, i) for i in range(levels - 1)])
    spacing = inverse_spacing[None, :, None, None, None]
    lower = jnp.concatenate((below, uw_hat[:, :-1]), axis=1)
    upper = jnp.concatenate((uw_hat[:, 1:], above), axis=1)
    slope_y = (upper - lower) * spacing

    u, w = to_x(uw_hat[0]), to_x(uw_hat[1])
    vort_y = to_x(dzu_hat - turned(uw_hat[1]))
    v = to_x(v_hat)
    vort_z = to_x(turned(v_hat) - slope_y[0])
    vort_x = to_x(slope_y[1] - dzv_hat)
    lamb = jnp.stack(
        (v * vort_z - w * vort_y, w * vort_x - u * vort_z, u * vort_y - v * vort_x)
    )
    local_peak = jnp.max(vort_x * vort_x + vort_y * vort_y + vort_z * vort_z)
    magnitude = jnp.sqrt(everywhere_max(local_peak, ("gy", "pa")))
    return (lamb / (magnitude + 1e-06), magnitude)


def solution(mesh):
    placed = (P(None, "gy", "pa", None), P("gy"))
    return jax.shard_map(
        body,
        mesh=mesh,
        in_specs=placed,
        out_specs=(P(None, "gy", "pa", None), P()),
        check_vma=False,
    )
```

time: 894 us -> 364 us (0.41)
  matrix products: 313 us -> 86.9 us
  waiting for transfers between devices: 314 us -> 116 us
  blocking collectives: 108 us -> 0 us
  starting transfers between devices: 11.1 us -> 112 us
  local copies, waits for them, and re-layouts: 87.1 us -> 13.7 us
  other arithmetic: 52.2 us -> 22.8 us
    all_to_all x1 -> x0, waiting for transfers between devices: 308 us -> none  [body(): lax.all_to_all(spectra, 'pa', split_axis=4, concat_axis=2, tiled=True)]
    dot_general x6 -> x10, matrix products: 313 us -> 86.9 us  [the longest x6 50.5 us: to_x(): jnp.einsum('...zm,mx->...zx', flat, table_x, precision=lax.Precision.HIGH...]
    ppermute x2 -> x19, waiting for transfers between devices: 5.81 us -> 116 us  [the longest x12 105 us: exchange(): lax.ppermute(block, 'pa', [(i, (i + shift) % parts) for i in range(parts)])]
    pmax x1 -> x0, blocking collectives: 108 us -> none  [body(): peak_square = lax.pmax(local_peak, ('gy', 'pa'))]
    ppermute x2 -> x19, starting transfers between devices: 4.54 us -> 112 us  [the longest x12 78.8 us: exchange(): lax.ppermute(block, 'pa', [(i, (i + shift) % parts) for i in range(parts)])]
    all_to_all x3 -> x0, local copies, waits for them, and re-layouts: 47.8 us -> none  [body(): lax.all_to_all(spectra, 'pa', split_axis=4, concat_axis=2, tiled=True)]
    another operation x1, local copies, waits for them, and re-layouts: 21.7 us -> 1.93 us  [to_z(): return jnp.stack((real_out, imag_out), axis=-2)]
    another operation x2 -> x0, other arithmetic: 19.6 us -> none  [the longest x1 11.4 us: to_z(): return jnp.stack((real_out, imag_out), axis=-2)]
  transfers between devices with their start and end apart: 3 -> 19, of which waited for: 3 -> 8; matrix products, arithmetic and copies ran while one was open for 0% -> 17% of each run, Pallas kernels for 0% -> 0%
where the time goes in v1:
time: 364 us; the launch traced here: 358 us
  waiting for transfers between devices  116 us (32%)
  starting transfers between devices  112 us (31%)
  matrix products  86.9 us (24%)
  other arithmetic  22.8 us (6%)
  local copies, waits for them, and re-layouts  13.7 us (4%)
  between operations  6.43 us (2%)
    ppermute x12, waiting for transfers between devices, exchange(): lax.ppermute(block, 'pa', [(i, (i + shift) % parts) for i in range(parts)])  105 us
    ppermute x12, starting transfers between devices, exchange(): lax.ppermute(block, 'pa', [(i, (i + shift) % parts) for i in range(parts)])  78.8 us
    dot_general x6, matrix products, to_x(): jnp.einsum('...zm,mx->...zx', flat, table_x, precision=lax.Precision.HIGH...  50.5 us
    dot_general x4, matrix products, exchange(): jnp.einsum('dnk,fjmk->dfjnm', table, modes, precision=lax.Precision.HIGH,...  36.4 us
    ppermute x5, starting transfers between devices, everywhere_max(): value = jnp.maximum(value, lax.ppermute(value, axis, pairs))  30.3 us
    ppermute x5, waiting for transfers between devices, everywhere_max(): value = jnp.maximum(value, lax.ppermute(value, axis, pairs))  11.3 us
    div x1, other arithmetic, body(): return (lamb / (magnitude + 1e-06), magnitude)  9.39 us
  transfers between devices with their start and end apart: 19, of which 8 were waited for; matrix products, arithmetic and copies ran while one was open for 17% of the time, Pallas kernels for 0%

profile of v1, /device:TPU:0, one launch (start us, length us, event | category | flops | bytes accessed | tf_op | source)
XLA Modules:
  0.0 357.9 jit_solution(10813896155509421837)
XLA Ops:
  0.7 9.3 %fusion.33 = f32[4,576,2,128]{3,1,2,0:T(8,128)S(1)} fusion(f32[4,576,1536,1]{2,1,3,0:T(8,128)} %constant.115, f32[3,2,128,1536]{3,2,1,0:T(8,128)} %param.7), kind=kOutput, calls=%fused_computation.51 | convolution fusion | flops 5435817984 | bytes 18087936 | tf_op jit(solution)/shard_map/dnk,fjmk->dfjnm/dot_general | solution.py:71
  11.5 4.0 %collective-permute-start.1 = (f32[1,2,576,128]{3,2,1,0:T(8,128)}, f32[1,2,576,128]{3,2,1,0:T(8,128)}, u32[]{:S(2)}, u32[]{:S(2)}) collective-permute-start(f32[1,2,576,128]{3,2,1,0:T(8,128)} %get-tuple-element.43), channel_id=1, source_target_pairs={{0,2},{1,3},{2,0},{3,1},{4,6},{5,7},{6,4},{7,5},{8,10},{9,11},{10,... | collective-permute-start | bytes 1769480 | tf_op jit(solution)/shard_map/ppermute | solution.py:78
  15.5 1.6 collective-permute-start
  17.3 14.3 %fusion.1 = f32[2,2,128,4,576]{2,4,3,1,0:T(8,128)S(1)} fusion(f32[4,576,1536,1,1]{2,1,0,4,3:T(8,128)} %constant.116, f32[1,2,128,1536]{3,2,1,0:T(8,128)S(1)} %get-tuple-element.17, f32[1,2,128,1536]{3,2,1,0:T(8,128)S(1)} %get-tuple-element.16), kind=kOutput, calls=%fused_computation.10 | convolution fusion | flops 10872422400 | bytes 22020096 | tf_op jit(solution)/shard_map/dnk,fjmk->dfjnm/dot_general | solution.py:71
  31.7 1.9 constant_dynamic-slice_fusion.2
  33.6 4.0 %collective-permute-start.5 = (f32[2,2,576,128]{3,2,1,0:T(8,128)}, f32[2,2,576,128]{3,2,1,0:T(8,128)}, u32[]{:S(2)}, u32[]{:S(2)}) collective-permute-start(f32[2,2,576,128]{3,2,1,0:T(8,128)} %get-tuple-element.14), channel_id=1, source_target_pairs={{0,3},{1,0},{2,1},{3,2},{4,7},{5,4},{6,5},{7,6},{8,11},{9,8},{10,9... | collective-permute-start | bytes 3538952 | tf_op jit(solution)/shard_map/ppermute | solution.py:78
  37.7 6.3 %fusion.32 = f32[4,576,2,128]{3,1,2,0:T(8,128)S(1)} fusion(f32[4,576,1536,1]{2,1,3,0:T(8,128)S(1)} %bitcast.236, f32[3,2,128,1536]{3,2,1,0:T(8,128)S(1)} %copy-done), kind=kOutput, calls=%fused_computation.50 | convolution fusion | flops 5435817984 | bytes 18087936 | tf_op jit(solution)/shard_map/dnk,fjmk->dfjnm/dot_general | solution.py:71
  44.0 6.4 %fusion.30 = f32[4,576,2,128]{3,1,2,0:T(8,128)S(1)} fusion(f32[4,576,1536,1]{2,1,3,0:T(8,128)S(1)} %bitcast.236, f32[3,2,128,1536]{3,2,1,0:T(8,128)S(1)} %copy-done), kind=kOutput, calls=%fused_computation.48 | convolution fusion | flops 5435817984 | bytes 18087936 | tf_op jit(solution)/shard_map/dnk,fjmk->dfjnm/dot_general | solution.py:71
  52.1 28.5 %collective-permute-done.1 = f32[1,2,576,128]{3,2,1,0:T(8,128)} collective-permute-done((f32[1,2,576,128]{3,2,1,0:T(8,128)}, f32[1,2,576,128]{3,2,1,0:T(8,128)}, u32[]{:S(2)}, u32[]{:S(2)}) %collective-permute-start.1) | collective-permute-done | bytes 589856 | tf_op jit(solution)/shard_map/ppermute | solution.py:78
  81.9 3.3 constant_dynamic-slice_fusion.3
  85.3 45.5 %collective-permute-done.2 = f32[1,2,576,128]{3,2,1,0:T(8,128)S(1)} collective-permute-done((f32[1,2,576,128]{3,2,1,0:T(8,128)}, f32[1,2,576,128]{3,2,1,0:T(8,128)S(1)}, u32[]{:S(2)}, u32[]{:S(2)}) %collective-permute-start.2) | collective-permute-done | bytes 589856 | tf_op jit(solution)/shard_map/ppermute | solution.py:78
  130.8 64.0 %collective-permute-start.11 = (f32[1,2,576,128]{3,2,1,0:T(8,128)}, f32[1,2,576,128]{3,2,1,0:T(8,128)}, u32[]{:S(2)}, u32[]{:S(2)}) collective-permute-start(f32[1,2,576,128]{3,2,1,0:T(8,128)} %get-tuple-element.38), channel_id=1, source_target_pairs={{0,1},{1,2},{2,3},{3,0},{4,5},{5,6},{6,7},{7,4},{8,9},{9,10},{10,1... | collective-permute-start | bytes 1769480 | tf_op jit(solution)/shard_map/ppermute | solution.py:78
  197.3 2.3 pad_maximum_fusion
  202.9 2.3 pad_maximum_fusion.1
  206.0 5.9 %fusion.26 = f32[2,288,1536]{2,1,0:T(8,128)S(1)} fusion(f32[1024,1536,1]{1,0,2:T(8,128)S(1)} %bitcast.229, f32[2,288,512]{2,1,0:T(8,128)S(1)} %get-tuple-element.33, f32[2,288,512]{2,1,0:T(8,128)S(1)} %get-tuple-element.32), kind=kOutput, calls=%fused_computation.43 | convolution fusion | flops 5436407808 | bytes 12189696 | tf_op jit(solution)/shard_map/...zm,mx->...zx/dot_general | solution.py:84
  212.1 7.8 %fusion.14 = f32[2,288,1536]{2,1,0:T(8,128)} fusion(f32[1024,1536,1]{1,0,2:T(8,128)S(1)} %bitcast.230, f32[2,288,512]{2,1,0:T(8,128)S(1)} %get-tuple-element.19, f32[2,288,512]{2,1,0:T(8,128)S(1)} %get-tuple-element.18), kind=kOutput, calls=%fused_computation.28 | convolution fusion | flops 5436407808 | bytes 12189696 | tf_op jit(solution)/shard_map/...zm,mx->...zx/dot_general | solution.py:84
  222.7 2.9 collective-permute-start.10
  226.3 3.7 %fusion = f32[2,2,2,288,512]{4,3,1,2,0:T(8,128)S(1)} fusion(f32[2,1,2,288,512]{4,3,1,2,0:T(8,128)} %collective-permute-done.6, f32[2,1,2,288,512]{4,3,1,2,0:T(8,128)S(1)} %get-tuple-element.10, f32[2,1,2,288,512]{4,3,1,2,0:T(8,128)S(1)} %get-tuple-element.11, f32[2,1,2,288,512]{4,3,1,2,0:T(8,128)} %copy-done.2, f32[2]{0:T(128)S(1)} %copy-done.5), kind=kLoop, calls=%fused_computation.3 | loop fusion | flops 4718592 | bytes 14155784 | tf_op jit(solution)/shard_map/mul | solution.py:103
  230.1 30.9 %collective-permute-done.9 = f32[1,2,576,128]{3,2,1,0:T(8,128)} collective-permute-done((f32[1,2,576,128]{3,2,1,0:T(8,128)}, f32[1,2,576,128]{3,2,1,0:T(8,128)}, u32[]{:S(2)}, u32[]{:S(2)}) %collective-permute-start.9) | collective-permute-done | bytes 589856 | tf_op jit(solution)/shard_map/ppermute | solution.py:78
  261.0 2.9 fusion.5
  264.6 7.7 %fusion.22 = f32[2,288,1536]{2,1,0:T(8,128)} fusion(f32[1024,1536,1]{1,0,2:T(8,128)S(1)} %bitcast.231, f32[2,288,512]{2,1,0:T(8,128)S(1)} %get-tuple-element.35, f32[2,288,512]{2,1,0:T(8,128)S(1)} %get-tuple-element.34), kind=kOutput, calls=%fused_computation.39 | convolution fusion | flops 5436407808 | bytes 12189696 | tf_op jit(solution)/shard_map/...zm,mx->...zx/dot_general | solution.py:84
  272.3 8.0 %fusion.18 = f32[2,288,1536]{2,1,0:T(8,128)} fusion(f32[1024,1536,1]{1,0,2:T(8,128)S(1)} %bitcast.232, f32[2,288,512]{2,1,0:T(8,128)S(1)} %get-tuple-element.25, f32[2,288,512]{2,1,0:T(8,128)S(1)} %get-tuple-element.24), kind=kOutput, calls=%fused_computation.34 | convolution fusion | flops 5436407808 | bytes 12189696 | tf_op jit(solution)/shard_map/...zm,mx->...zx/dot_general | solution.py:84
  280.3 7.7 %fusion.10 = f32[2,288,1536]{2,1,0:T(8,128)} fusion(f32[1024,1536,1]{1,0,2:T(8,128)S(1)} %bitcast.233, f32[2,288,512]{2,1,0:T(8,128)S(1)} %get-tuple-element.21, f32[2,288,512]{2,1,0:T(8,128)S(1)} %get-tuple-element.20), kind=kOutput, calls=%fused_computation.24 | convolution fusion | flops 5436407808 | bytes 12189696 | tf_op jit(solution)/shard_map/...zm,mx->...zx/dot_general | solution.py:84
  287.9 13.6 %add_reduce_fusion = (f32[]{:T(128)}, f32[1,2,288,1536]{3,2,1,0:T(8,128)}, f32[1,2,288,1536]{3,2,1,0:T(8,128)}, f32[1,2,288,1536]{3,2,1,0:T(8,128)}) fusion(f32[2,288,1536]{2,1,0:T(8,128)} %fusion.10, f32[2,288,1536]{2,1,0:T(8,128)} %fusion.18, f32[2,288,1536]{2,1,0:T(8,128)} %fusion.22, f32[2,288,1536]{2,1,0:T(8,128)S(1)} %fusion.26, ...), kind=kOutput, calls=%fused_computation.5 | convolution fusion | flops 5449678848 | bytes 36962308 | tf_op jit(solution)/shard_map/...zm,mx->...zx/dot_general | solution.py:84
  301.5 7.7 %collective-permute-start.14 = (f32[]{:T(128)}, f32[]{:T(128)}, u32[]{:S(2)}, u32[]{:S(2)}) collective-permute-start(f32[]{:T(128)} %get-tuple-element.2), channel_id=1, source_target_pairs={{0,4},{4,8},{8,12},{12,16},{16,20},{20,24},{24,28},{28,0},{1,5},{5... | collective-permute-start | bytes 20 | tf_op jit(solution)/shard_map/ppermute | solution.py:48
  311.4 13.4 %collective-permute-start.15 = (f32[]{:T(128)}, f32[]{:T(128)}, u32[]{:S(2)}, u32[]{:S(2)}) collective-permute-start(f32[]{:T(128)} %max.15), channel_id=1, source_target_pairs={{0,8},{4,12},{8,16},{12,20},{16,24},{20,28},{24,0},{28,4},{1,9},{5... | collective-permute-start | bytes 20 | tf_op jit(solution)/shard_map/ppermute | solution.py:48
  324.9 3.7 %collective-permute-done.15 = f32[]{:T(128)} collective-permute-done((f32[]{:T(128)}, f32[]{:T(128)}, u32[]{:S(2)}, u32[]{:S(2)}) %collective-permute-start.15) | collective-permute-done | bytes 36 | tf_op jit(solution)/shard_map/ppermute | solution.py:48
  329.2 5.9 %collective-permute-start.16 = (f32[]{:T(128)}, f32[]{:T(128)}, u32[]{:S(2)}, u32[]{:S(2)}) collective-permute-start(f32[]{:T(128)} %max.16), channel_id=1, source_target_pairs={{0,16},{4,20},{8,24},{12,28},{16,0},{20,4},{24,8},{28,12},{1,17},{... | collective-permute-start | bytes 20 | tf_op jit(solution)/shard_map/ppermute | solution.py:48
  336.0 1.9 collective-permute-start.17
  337.9 3.4 collective-permute-done.17
  343.3 3.1 collective-permute-done.18
  347.2 9.4 %maximum_divide_fusion = f32[3,2,288,1536]{3,2,1,0:T(8,128)} fusion(f32[1,2,288,1536]{3,2,1,0:T(8,128)} %get-tuple-element.3, f32[1,2,288,1536]{3,2,1,0:T(8,128)} %get-tuple-element.4, f32[1,2,288,1536]{3,2,1,0:T(8,128)} %get-tuple-element.5, f32[]{:T(128)S(6)} %add.124), kind=kLoop, calls=%fused_computation | loop fusion | flops 7962624 | bytes 21233668 | tf_op jit(solution)/shard_map/div | solution.py:115
  (61 shorter events, 18.1 us)
Async XLA Ops:
  10.0 7.1 %copy-start = (f32[3,2,128,1536]{3,2,1,0:T(8,128)S(1)}, f32[3,2,128,1536]{3,2,1,0:T(8,128)}, u32[]{:S(2)}) copy-start(f32[3,2,128,1536]{3,2,1,0:T(8,128)} %param.7) | copy-start | bytes 14155780
  11.5 69.1 %collective-permute-start.1 = (f32[1,2,576,128]{3,2,1,0:T(8,128)}, f32[1,2,576,128]{3,2,1,0:T(8,128)}, u32[]{:S(2)}, u32[]{:S(2)}) collective-permute-start(f32[1,2,576,128]{3,2,1,0:T(8,128)} %get-tuple-element.43), channel_id=1, source_target_pairs={{0,2},{1,3},{2,0},{3,1},{4,6},{5,7},{6,4},{7,5},{8,10},{9,11},{10,... | collective-permute-start | bytes 1769480 | tf_op jit(solution)/shard_map/ppermute | solution.py:78
  15.5 69.7 %collective-permute-start = (f32[1,2,576,128]{3,2,1,0:T(8,128)}, f32[1,2,576,128]{3,2,1,0:T(8,128)}, u32[]{:S(2)}, u32[]{:S(2)}) collective-permute-start(f32[1,2,576,128]{3,2,1,0:T(8,128)} %get-tuple-element.44), channel_id=1, source_target_pairs={{0,1},{1,2},{2,3},{3,0},{4,5},{5,6},{6,7},{7,4},{8,9},{9,10},{10,1... | collective-permute-start | bytes 1769480 | tf_op jit(solution)/shard_map/ppermute | solution.py:78
  17.3 20.3 %slice-start = ((s8[14155776]{0:T(1024)(128)(4,1)}), s8[4194304]{0:T(1024)(128)(4,1)S(1)}, s32[]{:S(2)}) async-start(s8[14155776]{0:T(1024)(128)(4,1)} %bitcast.235), calls=%async_computation | async-start | bytes 8388608
  17.3 20.3 %slice-start.1 = ((s8[14155776]{0:T(1024)(128)(4,1)}), s8[4194304]{0:T(1024)(128)(4,1)S(1)}, s32[]{:S(2)}) async-start(s8[14155776]{0:T(1024)(128)(4,1)} %bitcast.235), calls=%async_computation.1 | async-start | bytes 8388608
  17.3 20.3 %slice-start.2 = ((s8[14155776]{0:T(1024)(128)(4,1)}), s8[1572864]{0:T(1024)(128)(4,1)S(1)}, s32[]{:S(2)}) async-start(s8[14155776]{0:T(1024)(128)(4,1)} %bitcast.235), calls=%async_computation.2 | async-start | bytes 3145728
  31.7 6.0 %slice-start.3 = ((s8[14155776]{0:T(1024)(128)(4,1)}), s8[4194304]{0:T(1024)(128)(4,1)S(1)}, s32[]{:S(2)}) async-start(s8[14155776]{0:T(1024)(128)(4,1)} %bitcast.235), calls=%async_computation.3 | async-start | bytes 8388608
  33.6 162.8 %collective-permute-start.3 = (f32[2,2,576,128]{3,2,1,0:T(8,128)}, f32[2,2,576,128]{3,2,1,0:T(8,128)}, u32[]{:S(2)}, u32[]{:S(2)}) collective-permute-start(f32[2,2,576,128]{3,2,1,0:T(8,128)} %get-tuple-element.13), channel_id=1, source_target_pairs={{0,1},{1,2},{2,3},{3,0},{4,5},{5,6},{6,7},{7,4},{8,9},{9,10},{10,1... | collective-permute-start | bytes 3538952 | tf_op jit(solution)/shard_map/ppermute | solution.py:78
  33.6 163.7 %collective-permute-start.5 = (f32[2,2,576,128]{3,2,1,0:T(8,128)}, f32[2,2,576,128]{3,2,1,0:T(8,128)}, u32[]{:S(2)}, u32[]{:S(2)}) collective-permute-start(f32[2,2,576,128]{3,2,1,0:T(8,128)} %get-tuple-element.14), channel_id=1, source_target_pairs={{0,3},{1,0},{2,1},{3,2},{4,7},{5,4},{6,5},{7,6},{8,11},{9,8},{10,9... | collective-permute-start | bytes 3538952 | tf_op jit(solution)/shard_map/ppermute | solution.py:78
  37.6 159.7 %collective-permute-start.4 = (f32[2,2,576,128]{3,2,1,0:T(8,128)}, f32[2,2,576,128]{3,2,1,0:T(8,128)}, u32[]{:S(2)}, u32[]{:S(2)}) collective-permute-start(f32[2,2,576,128]{3,2,1,0:T(8,128)} %get-tuple-element.15), channel_id=1, source_target_pairs={{0,2},{1,3},{2,0},{3,1},{4,6},{5,7},{6,4},{7,5},{8,10},{9,11},{10,... | collective-permute-start | bytes 3538952 | tf_op jit(solution)/shard_map/ppermute | solution.py:78
  80.6 50.2 %collective-permute-start.2 = (f32[1,2,576,128]{3,2,1,0:T(8,128)}, f32[1,2,576,128]{3,2,1,0:T(8,128)S(1)}, u32[]{:S(2)}, u32[]{:S(2)}) collective-permute-start(f32[1,2,576,128]{3,2,1,0:T(8,128)} %get-tuple-element.45), channel_id=1, source_target_pairs={{0,3},{1,0},{2,1},{3,2},{4,7},{5,4},{6,5},{7,6},{8,11},{9,8},{10,9... | collective-permute-start | bytes 1769480 | tf_op jit(solution)/shard_map/ppermute | solution.py:78
  81.9 112.9 %copy-start.1 = (f32[1,576,2,128]{3,1,2,0:T(8,128)S(1)}, f32[1,576,2,128]{3,1,2,0:T(8,128)}, u32[]{:S(2)}) copy-start(f32[1,576,2,128]{3,1,2,0:T(8,128)} %get-tuple-element.42) | copy-start | bytes 1769476
  85.2 134.7 %collective-permute-start.12 = (f32[1,2,576,128]{3,2,1,0:T(8,128)}, f32[1,2,576,128]{3,2,1,0:T(8,128)}, u32[]{:S(2)}, u32[]{:S(2)}) collective-permute-start(f32[1,2,576,128]{3,2,1,0:T(8,128)} %get-tuple-element.37), channel_id=1, source_target_pairs={{0,2},{1,3},{2,0},{3,1},{4,6},{5,7},{6,4},{7,5},{8,10},{9,11},{10,... | collective-permute-start | bytes 1769480 | tf_op jit(solution)/shard_map/ppermute | solution.py:78
  130.8 99.3 %collective-permute-start.11 = (f32[1,2,576,128]{3,2,1,0:T(8,128)}, f32[1,2,576,128]{3,2,1,0:T(8,128)}, u32[]{:S(2)}, u32[]{:S(2)}) collective-permute-start(f32[1,2,576,128]{3,2,1,0:T(8,128)} %get-tuple-element.38), channel_id=1, source_target_pairs={{0,1},{1,2},{2,3},{3,0},{4,5},{5,6},{6,7},{7,4},{8,9},{9,10},{10,1... | collective-permute-start | bytes 1769480 | tf_op jit(solution)/shard_map/ppermute | solution.py:78
  196.2 1.1 copy-start.4
  197.3 32.8 %collective-permute-start.13 = (f32[1,2,576,128]{3,2,1,0:T(8,128)S(1)}, f32[1,2,576,128]{3,2,1,0:T(8,128)}, u32[]{:S(2)}, u32[]{:S(2)}) collective-permute-start(f32[1,2,576,128]{3,2,1,0:T(8,128)S(1)} %copy-done.4), channel_id=1, source_target_pairs={{0,3},{1,0},{2,1},{3,2},{4,7},{5,4},{6,5},{7,6},{8,11},{9,8},{10,9... | collective-permute-start | bytes 1769480 | tf_op jit(solution)/shard_map/ppermute | solution.py:78
  200.2 21.1 %collective-permute-start.7 = (f32[2,1,2,288,512]{4,3,1,2,0:T(8,128)S(1)}, f32[2,1,2,288,512]{4,3,1,2,0:T(8,128)S(1)}, u32[]{:S(2)}, u32[]{:S(2)}) collective-permute-start(f32[2,1,2,288,512]{4,3,1,2,0:T(8,128)S(1)} %get-tuple-element.10), channel_id=1, source_target_pairs={{0,4},{4,8},{8,12},{12,16},{16,20},{20,24},{24,28},{1,5},{5,9},{9,... | collective-permute-start | bytes 7077896 | tf_op jit(solution)/shard_map/ppermute | solution.py:98
  201.6 20.3 %collective-permute-start.6 = (f32[2,1,2,288,512]{4,3,1,2,0:T(8,128)S(1)}, f32[2,1,2,288,512]{4,3,1,2,0:T(8,128)}, u32[]{:S(2)}, u32[]{:S(2)}) collective-permute-start(f32[2,1,2,288,512]{4,3,1,2,0:T(8,128)S(1)} %get-tuple-element.11), channel_id=1, source_target_pairs={{4,0},{8,4},{12,8},{16,12},{20,16},{24,20},{28,24},{5,1},{9,5},{13... | collective-permute-start | bytes 7077896 | tf_op jit(solution)/shard_map/ppermute | solution.py:99
  219.9 41.1 %collective-permute-start.9 = (f32[1,2,576,128]{3,2,1,0:T(8,128)}, f32[1,2,576,128]{3,2,1,0:T(8,128)}, u32[]{:S(2)}, u32[]{:S(2)}) collective-permute-start(f32[1,2,576,128]{3,2,1,0:T(8,128)} %get-tuple-element.27), channel_id=1, source_target_pairs={{0,2},{1,3},{2,0},{3,1},{4,6},{5,7},{6,4},{7,5},{8,10},{9,11},{10,... | collective-permute-start | bytes 1769480 | tf_op jit(solution)/shard_map/ppermute | solution.py:78
  221.3 1.4 copy-start.2
  221.3 39.7 %collective-permute-start.8 = (f32[1,2,576,128]{3,2,1,0:T(8,128)}, f32[1,2,576,128]{3,2,1,0:T(8,128)}, u32[]{:S(2)}, u32[]{:S(2)}) collective-permute-start(f32[1,2,576,128]{3,2,1,0:T(8,128)} %get-tuple-element.28), channel_id=1, source_target_pairs={{0,1},{1,2},{2,3},{3,0},{4,5},{5,6},{6,7},{7,4},{8,9},{9,10},{10,1... | collective-permute-start | bytes 1769480 | tf_op jit(solution)/shard_map/ppermute | solution.py:78
  222.7 3.6 copy-start.5
  222.7 38.3 %collective-permute-start.10 = (f32[1,2,576,128]{3,2,1,0:T(8,128)}, f32[1,2,576,128]{3,2,1,0:T(8,128)}, u32[]{:S(2)}, u32[]{:S(2)}) collective-permute-start(f32[1,2,576,128]{3,2,1,0:T(8,128)} %get-tuple-element.29), channel_id=1, source_target_pairs={{0,3},{1,0},{2,1},{3,2},{4,7},{5,4},{6,5},{7,6},{8,11},{9,8},{10,9... | collective-permute-start | bytes 1769480 | tf_op jit(solution)/shard_map/ppermute | solution.py:78
  226.3 34.7 %copy-start.3 = (f32[1,576,2,128]{3,1,2,0:T(8,128)S(1)}, f32[1,576,2,128]{3,1,2,0:T(8,128)}, u32[]{:S(2)}) copy-start(f32[1,576,2,128]{3,1,2,0:T(8,128)} %get-tuple-element.36) | copy-start | bytes 1769476
  301.5 8.6 %collective-permute-start.14 = (f32[]{:T(128)}, f32[]{:T(128)}, u32[]{:S(2)}, u32[]{:S(2)}) collective-permute-start(f32[]{:T(128)} %get-tuple-element.2), channel_id=1, source_target_pairs={{0,4},{4,8},{8,12},{12,16},{16,20},{20,24},{24,28},{28,0},{1,5},{5... | collective-permute-start | bytes 20 | tf_op jit(solution)/shard_map/ppermute | solution.py:48
  311.4 17.1 %collective-permute-start.15 = (f32[]{:T(128)}, f32[]{:T(128)}, u32[]{:S(2)}, u32[]{:S(2)}) collective-permute-start(f32[]{:T(128)} %max.15), channel_id=1, source_target_pairs={{0,8},{4,12},{8,16},{12,20},{16,24},{20,28},{24,0},{28,4},{1,9},{5... | collective-permute-start | bytes 20 | tf_op jit(solution)/shard_map/ppermute | solution.py:48
  329.2 6.1 %collective-permute-start.16 = (f32[]{:T(128)}, f32[]{:T(128)}, u32[]{:S(2)}, u32[]{:S(2)}) collective-permute-start(f32[]{:T(128)} %max.16), channel_id=1, source_target_pairs={{0,16},{4,20},{8,24},{12,28},{16,0},{20,4},{24,8},{28,12},{1,17},{... | collective-permute-start | bytes 20 | tf_op jit(solution)/shard_map/ppermute | solution.py:48
  336.0 5.3 %collective-permute-start.17 = (f32[]{:T(128)}, f32[]{:T(128)}, u32[]{:S(2)}, u32[]{:S(2)}) collective-permute-start(f32[]{:T(128)} %max.17), channel_id=1, source_target_pairs={{0,1},{1,2},{2,3},{3,0},{4,5},{5,6},{6,7},{7,4},{8,9},{9,10},{10,1... | collective-permute-start | bytes 20 | tf_op jit(solution)/shard_map/ppermute | solution.py:48
  342.0 4.5 %collective-permute-start.18 = (f32[]{:T(128)}, f32[]{:T(128)}, u32[]{:S(2)}, u32[]{:S(2)}) collective-permute-start(f32[]{:T(128)} %max.18), channel_id=1, source_target_pairs={{0,2},{1,3},{2,0},{3,1},{4,6},{5,7},{6,4},{7,5},{8,10},{9,11},{10,... | collective-permute-start | bytes 20 | tf_op jit(solution)/shard_map/ppermute | solution.py:48

commit v2 on v1

--- a/solution.py
+++ b/solution.py
@@ -67,17 +67,23 @@
     kx = (order[:, None] * kx_local + jnp.arange(kx_local)[None, :]).reshape(-1)
     wave_x = kx.astype(jnp.float32) * (2.0 * math.pi / NX)
 
-    def exchange(modes, table):
+    def synthesized(modes, table):
         out = jnp.einsum(
             "dnk,fjmk->dfjnm", table, modes, precision=lax.Precision.HIGH,
             preferred_element_type=jnp.float32,
         )
-        got = [lax.dynamic_index_in_dim(out, me, 0, keepdims=False)]
+        return [
+            lax.dynamic_index_in_dim(out, (me + shift) % parts, 0, keepdims=False)
+            for shift in range(parts)
+        ]
+
+    def exchange(blocks):
+        got = [blocks[0]]
         for shift in range(1, parts):
-            block = lax.dynamic_index_in_dim(out, (me + shift) % parts, 0, keepdims=False)
-            got.append(lax.ppermute(block, "pa", [(i, (i + shift) % parts) for i in range(parts)]))
+            pairs = [(i, (i + shift) % parts) for i in range(parts)]
+            got.append(lax.ppermute(blocks[shift], "pa", pairs))
         whole = jnp.concatenate(got, axis=-1)
-        return whole.reshape(whole.shape[:2] + (2, slab, KX))
+        return whole.reshape(whole.shape[:2] + (2, slab, KX)), got[1:]
 
     def to_x(hat):
         flat = jnp.concatenate((hat[..., 0, :, :], hat[..., 1, :, :]), axis=-1)
@@ -89,21 +95,26 @@
     def turned(hat):
         return jnp.stack((-wave_x * hat[..., 1, :, :], wave_x * hat[..., 0, :, :]), axis=-3)
 
+    def edges(hat):
+        below = lax.ppermute(hat[:, -1:], "gy", [(i, i + 1) for i in range(levels - 1)])
+        above = lax.ppermute(hat[:, :1], "gy", [(i + 1, i) for i in range(levels - 1)])
+        lower = jnp.concatenate((below, hat[:, :-1]), axis=1)
+        upper = jnp.concatenate((hat[:, 1:], above), axis=1)
+        return (upper - lower) * inverse_spacing[None, :, None, None, None]
+
     u_modes, v_modes, w_modes = (spectral_velocity[c : c + 1] for c in range(3))
-    uw_hat = exchange(jnp.concatenate((u_modes, w_modes)), plain)
-    dzu_hat = exchange(u_modes, slope)[0]
-    v_hat = exchange(v_modes, plain)[0]
-    dzv_hat = exchange(v_modes, slope)[0]
+    first = synthesized(jnp.concatenate((u_modes, w_modes)), plain)
+    pair_hat, got_pair = exchange(first)
+    (u_late, v_late), _ = lax.optimization_barrier(((u_modes, v_modes), first))
+    second = zip(synthesized(u_late, slope), synthesized(v_late, plain))
+    second_hat, _ = exchange([jnp.concatenate(both) for both in second])
+    last, _ = lax.optimization_barrier((synthesized(v_late, slope), got_pair))
+    dzv_hat = exchange(last)[0][0]
+    (u_hat, w_hat), (dzu_hat, v_hat) = pair_hat, second_hat
+    slope_y = edges(pair_hat)
 
-    below = lax.ppermute(uw_hat[:, -1:], "gy", [(i, i + 1) for i in range(levels - 1)])
-    above = lax.ppermute(uw_hat[:, :1], "gy", [(i + 1, i) for i in range(levels - 1)])
-    spacing = inverse_spacing[None, :, None, None, None]
-    lower = jnp.concatenate((below, uw_hat[:, :-1]), axis=1)
-    upper = jnp.concatenate((uw_hat[:, 1:], above), axis=1)
-    slope_y = (upper - lower) * spacing
-
-    u, w = to_x(uw_hat[0]), to_x(uw_hat[1])
-    vort_y = to_x(dzu_hat - turned(uw_hat[1]))
+    u, w = to_x(u_hat), to_x(w_hat)
+    vort_y = to_x(dzu_hat - turned(w_hat))
     v = to_x(v_hat)
     vort_z = to_x(turned(v_hat) - slope_y[0])
     vort_x = to_x(slope_y[1] - dzv_hat)

time: 364 us -> 392 us (1.077)
  starting transfers between devices: 112 us -> 148 us
  waiting for transfers between devices: 116 us -> 104 us
  other arithmetic: 22.8 us -> 27.2 us
    ppermute x14 -> x11, starting transfers between devices: 81.5 us -> 113 us  [the longest x9 108 us: exchange(): got.append(lax.ppermute(blocks[shift], 'pa', pairs))]
    ppermute x14 -> x11, waiting for transfers between devices: 105 us -> 95.6 us  [the longest x9 95.6 us: exchange(): got.append(lax.ppermute(blocks[shift], 'pa', pairs))]
    ppermute x5, starting transfers between devices: 30.3 us -> 35.6 us  [everywhere_max(): value = jnp.maximum(value, lax.ppermute(value, axis, pairs))]
    squeeze x0 -> x3, local copies, waits for them, and re-layouts: none -> 4.79 us  [synthesized(): lax.dynamic_index_in_dim(out, (me + shift) % parts, 0, keepdims=False)]
    unnamed x24 -> x31, local copies, waits for them, and re-layouts: 6.45 us -> 1.82 us
    concatenate x3 -> x4, other arithmetic: 6.02 us -> 8.31 us  [exchange(): whole = jnp.concatenate(got, axis=-1)]
  transfers between devices with their start and end apart: 19 -> 16, of which waited for: 8 -> 7; matrix products, arithmetic and copies ran while one was open for 17% -> 16% of each run, Pallas kernels for 0% -> 0%
where the time goes in v2:
time: 392 us; the launch traced here: 388 us
  starting transfers between devices  148 us (38%)
  waiting for transfers between devices  104 us (27%)
  matrix products  85.7 us (22%)
  other arithmetic  27.2 us (7%)
  local copies, waits for them, and re-layouts  16.1 us (4%)
  between operations  6.5 us (2%)
    ppermute x9, starting transfers between devices, exchange(): got.append(lax.ppermute(blocks[shift], 'pa', pairs))  108 us
    ppermute x9, waiting for transfers between devices, exchange(): got.append(lax.ppermute(blocks[shift], 'pa', pairs))  95.6 us
    dot_general x6, matrix products, to_x(): jnp.einsum('...zm,mx->...zx', flat, table_x, precision=lax.Precision.HIGH...  51 us
    ppermute x5, starting transfers between devices, everywhere_max(): value = jnp.maximum(value, lax.ppermute(value, axis, pairs))  35.6 us
    dot_general x4, matrix products, synthesized(): jnp.einsum('dnk,fjmk->dfjnm', table, modes, precision=lax.Precision.HIGH,...  34.8 us
    div x1, other arithmetic, body(): return (lamb / (magnitude + 1e-06), magnitude)  9.39 us
    ppermute x5, waiting for transfers between devices, everywhere_max(): value = jnp.maximum(value, lax.ppermute(value, axis, pairs))  8.51 us
    concatenate x4, other arithmetic, exchange(): whole = jnp.concatenate(got, axis=-1)  8.31 us
  transfers between devices with their start and end apart: 16, of which 7 were waited for; matrix products, arithmetic and copies ran while one was open for 16% of the time, Pallas kernels for 0%

profile of v2, /device:TPU:0, one launch (start us, length us, event | category | flops | bytes accessed | tf_op | source)
XLA Modules:
  0.0 387.8 jit_solution(2086552004766321874)
XLA Ops:
  0.7 3.9 %fusion.48 = (f32[1,2,128,1536]{3,2,1,0:T(8,128)}, f32[1,2,128,1536]{3,2,1,0:T(8,128)S(1)}, f32[1,2,128,1536]{3,2,1,0:T(8,128)S(1)}) fusion(f32[3,2,128,1536]{3,2,1,0:T(8,128)} %param.7), kind=kLoop, calls=%fused_computation.104 | loop fusion | bytes 9437184 | tf_op jit(solution)/shard_map/slice | solution.py:105
  5.8 14.6 %fusion.1 = f32[2,2,128,4,576]{2,4,3,1,0:T(8,128)S(1)} fusion(f32[4,576,1536,1,1]{2,1,0,4,3:T(8,128)} %constant.125, f32[1,2,128,1536]{3,2,1,0:T(8,128)} %get-tuple-element.30, f32[1,2,128,1536]{3,2,1,0:T(8,128)S(1)} %get-tuple-element.8), kind=kOutput, calls=%fused_computation.11 | convolution fusion | flops 10872422400 | bytes 22020096 | tf_op jit(solution)/shard_map/dnk,fjmk->dfjnm/dot_general | solution.py:71
  20.4 1.9 dynamic-slice_bitcast_fusion
  22.4 5.0 %collective-permute-start.5 = (f32[2,2,576,128]{3,2,1,0:T(8,128)}, f32[2,2,576,128]{3,2,1,0:T(8,128)}, u32[]{:S(2)}, u32[]{:S(2)}) collective-permute-start(f32[2,2,576,128]{3,2,1,0:T(8,128)} %get-tuple-element.26), channel_id=1, source_target_pairs={{0,3},{1,0},{2,1},{3,2},{4,7},{5,4},{6,5},{7,6},{8,11},{9,8},{10,9... | collective-permute-start | bytes 3538952 | tf_op jit(solution)/shard_map/ppermute | solution.py:84
  28.7 6.5 %fusion.30 = f32[2,128,4,576]{1,3,2,0:T(8,128)S(1)} fusion(f32[4,576,1536,1]{2,1,0,3:T(8,128)S(1)} %bitcast.210, f32[1,2,128,1536]{3,2,1,0:T(8,128)S(1)} %copy-done.1), kind=kOutput, calls=%fused_computation.46 | convolution fusion | flops 5435817984 | bytes 18087936 | tf_op jit(solution)/shard_map/dnk,fjmk->dfjnm/dot_general | solution.py:71
  36.8 7.1 %fusion.32 = f32[2,128,4,576]{1,3,2,0:T(8,128)S(1)} fusion(f32[4,576,1536,1]{2,1,0,3:T(8,128)S(1)} %bitcast.210, f32[1,2,128,1536]{3,2,1,0:T(8,128)S(1)} %get-tuple-element.9), kind=kOutput, calls=%fused_computation.48 | convolution fusion | flops 5435817984 | bytes 18087936 | tf_op jit(solution)/shard_map/dnk,fjmk->dfjnm/dot_general | solution.py:71
  44.0 6.5 %fusion.34 = f32[2,128,4,576]{1,3,2,0:T(8,128)S(1)} fusion(f32[4,576,1536,1]{2,1,0,3:T(8,128)S(1)} %bitcast.216, f32[1,2,128,1536]{3,2,1,0:T(8,128)S(1)} %get-tuple-element.9), kind=kOutput, calls=%fused_computation.50 | convolution fusion | flops 5435817984 | bytes 18087936 | tf_op jit(solution)/shard_map/dnk,fjmk->dfjnm/dot_general | solution.py:71
  53.0 2.8 collective-permute-start.2
  56.9 2.0 collective-permute-start.1
  60.1 44.0 %collective-permute-start = (f32[2,2,576,128]{3,2,1,0:T(8,128)}, f32[2,2,576,128]{3,2,1,0:T(8,128)}, u32[]{:S(2)}, u32[]{:S(2)}) collective-permute-start(f32[2,2,576,128]{3,2,1,0:T(8,128)} %pad_maximum_fusion.4), channel_id=1, source_target_pairs={{0,1},{1,2},{2,3},{3,0},{4,5},{5,6},{6,7},{7,4},{8,9},{9,10},{10,1... | collective-permute-start | bytes 3538952 | tf_op jit(solution)/shard_map/ppermute | solution.py:84
  104.2 3.3 constant_dynamic-slice_fusion
  107.6 23.5 %collective-permute-done.4 = f32[2,2,576,128]{3,2,1,0:T(8,128)} collective-permute-done((f32[2,2,576,128]{3,2,1,0:T(8,128)}, f32[2,2,576,128]{3,2,1,0:T(8,128)}, u32[]{:S(2)}, u32[]{:S(2)}) %collective-permute-start.4) | collective-permute-done | bytes 1179680 | tf_op jit(solution)/shard_map/ppermute | solution.py:84
  131.0 49.8 %collective-permute-start.8 = (f32[1,2,576,128]{3,2,1,0:T(8,128)}, f32[1,2,576,128]{3,2,1,0:T(8,128)}, u32[]{:S(2)}, u32[]{:S(2)}) collective-permute-start(f32[1,2,576,128]{3,2,1,0:T(8,128)} %get-tuple-element.11), channel_id=1, source_target_pairs={{0,1},{1,2},{2,3},{3,0},{4,5},{5,6},{6,7},{7,4},{8,9},{9,10},{10,1... | collective-permute-start | bytes 1769480 | tf_op jit(solution)/shard_map/ppermute | solution.py:84
  180.8 3.4 collective-permute-start.9
  184.2 72.1 %collective-permute-done.1 = f32[2,2,576,128]{3,2,1,0:T(8,128)} collective-permute-done((f32[2,2,576,128]{3,2,1,0:T(8,128)}, f32[2,2,576,128]{3,2,1,0:T(8,128)}, u32[]{:S(2)}, u32[]{:S(2)}) %collective-permute-start.1) | collective-permute-done | bytes 1179680 | tf_op jit(solution)/shard_map/ppermute | solution.py:84
  256.4 2.2 pad_maximum_fusion
  259.3 2.3 pad_maximum_fusion.1
  262.1 2.7 collective-permute-start.7
  266.3 2.3 pad_maximum_fusion.2
  270.8 5.9 %fusion.18 = f32[2,288,1536]{2,1,0:T(8,128)S(1)} fusion(f32[1024,1536,1]{1,0,2:T(8,128)S(1)} %bitcast.203, f32[2,288,512]{2,1,0:T(8,128)S(1)} %get-tuple-element.40, f32[2,288,512]{2,1,0:T(8,128)S(1)} %get-tuple-element.39), kind=kOutput, calls=%fused_computation.33 | convolution fusion | flops 5436407808 | bytes 12189696 | tf_op jit(solution)/shard_map/...zm,mx->...zx/dot_general | solution.py:90
  276.6 7.9 %fusion.14 = f32[2,288,1536]{2,1,0:T(8,128)} fusion(f32[1024,1536,1]{1,0,2:T(8,128)S(1)} %bitcast.204, f32[2,288,512]{2,1,0:T(8,128)S(1)} %get-tuple-element.34, f32[2,288,512]{2,1,0:T(8,128)S(1)} %get-tuple-element.33), kind=kOutput, calls=%fused_computation.28 | convolution fusion | flops 5436407808 | bytes 12189696 | tf_op jit(solution)/shard_map/...zm,mx->...zx/dot_general | solution.py:90
  284.7 7.6 %fusion.6 = f32[2,288,1536]{2,1,0:T(8,128)} fusion(f32[1024,1536,1]{1,0,2:T(8,128)S(1)} %bitcast.205, f32[2,288,512]{2,1,0:T(8,128)S(1)} %get-tuple-element.52, f32[2,288,512]{2,1,0:T(8,128)S(1)} %get-tuple-element.51), kind=kOutput, calls=%fused_computation.20 | convolution fusion | flops 5436407808 | bytes 12189696 | tf_op jit(solution)/shard_map/...zm,mx->...zx/dot_general | solution.py:90
  294.0 3.7 fusion
  299.2 8.2 %fusion.22 = f32[2,288,1536]{2,1,0:T(8,128)} fusion(f32[1024,1536,1]{1,0,2:T(8,128)S(1)} %bitcast.206, f32[2,288,512]{2,1,0:T(8,128)S(1)} %get-tuple-element.46, f32[2,288,512]{2,1,0:T(8,128)S(1)} %get-tuple-element.45), kind=kOutput, calls=%fused_computation.38 | convolution fusion | flops 5436407808 | bytes 12189696 | tf_op jit(solution)/shard_map/...zm,mx->...zx/dot_general | solution.py:90
  307.4 7.7 %fusion.10 = f32[2,288,1536]{2,1,0:T(8,128)} fusion(f32[1024,1536,1]{1,0,2:T(8,128)S(1)} %bitcast.207, f32[2,288,512]{2,1,0:T(8,128)S(1)} %get-tuple-element.36, f32[2,288,512]{2,1,0:T(8,128)S(1)} %get-tuple-element.35), kind=kOutput, calls=%fused_computation.24 | convolution fusion | flops 5436407808 | bytes 12189696 | tf_op jit(solution)/shard_map/...zm,mx->...zx/dot_general | solution.py:90
  315.1 13.7 %add_reduce_fusion = (f32[]{:T(128)}, f32[1,2,288,1536]{3,2,1,0:T(8,128)}, f32[1,2,288,1536]{3,2,1,0:T(8,128)}, f32[1,2,288,1536]{3,2,1,0:T(8,128)}) fusion(f32[2,288,1536]{2,1,0:T(8,128)} %fusion.10, f32[2,288,1536]{2,1,0:T(8,128)S(1)} %fusion.18, f32[2,288,1536]{2,1,0:T(8,128)} %fusion.22, f32[2,288,1536]{2,1,0:T(8,128)} %fusion.6, ...), kind=kOutput, calls=%fused_computation.6 | convolution fusion | flops 5449678848 | bytes 36962308 | tf_op jit(solution)/shard_map/...zm,mx->...zx/dot_general | solution.py:90
  328.8 24.5 %collective-permute-start.11 = (f32[]{:T(128)}, f32[]{:T(128)}, u32[]{:S(2)}, u32[]{:S(2)}) collective-permute-start(f32[]{:T(128)} %get-tuple-element.14), channel_id=1, source_target_pairs={{0,4},{4,8},{8,12},{12,16},{16,20},{20,24},{24,28},{28,0},{1,5},{5... | collective-permute-start | bytes 20 | tf_op jit(solution)/shard_map/ppermute | solution.py:48
  355.6 3.3 collective-permute-start.12
  360.8 4.3 %collective-permute-start.13 = (f32[]{:T(128)}, f32[]{:T(128)}, u32[]{:S(2)}, u32[]{:S(2)}) collective-permute-start(f32[]{:T(128)} %max.16), channel_id=1, source_target_pairs={{0,16},{4,20},{8,24},{12,28},{16,0},{20,4},{24,8},{28,12},{1,17},{... | collective-permute-start | bytes 20 | tf_op jit(solution)/shard_map/ppermute | solution.py:48
  367.6 3.6 collective-permute-done.14
  373.8 2.6 collective-permute-done.15
  377.1 9.4 %maximum_divide_fusion = f32[3,2,288,1536]{3,2,1,0:T(8,128)} fusion(f32[1,2,288,1536]{3,2,1,0:T(8,128)} %get-tuple-element.15, f32[1,2,288,1536]{3,2,1,0:T(8,128)} %get-tuple-element.16, f32[1,2,288,1536]{3,2,1,0:T(8,128)} %get-tuple-element.17, f32[]{:T(128)S(6)} %add.131), kind=kLoop, calls=%fused_computation | loop fusion | flops 7962624 | bytes 21233668 | tf_op jit(solution)/shard_map/div | solution.py:126
  (71 shorter events, 22.9 us)
Async XLA Ops:
  4.6 1.2 copy-start
  5.8 22.9 %slice-start = ((s8[14155776]{0:T(1024)(128)(4,1)}), s8[4194304]{0:T(1024)(128)(4,1)S(1)}, s32[]{:S(2)}) async-start(s8[14155776]{0:T(1024)(128)(4,1)} %bitcast.209), calls=%async_computation | async-start | bytes 8388608
  5.8 22.9 %slice-start.1 = ((s8[14155776]{0:T(1024)(128)(4,1)}), s8[4194304]{0:T(1024)(128)(4,1)S(1)}, s32[]{:S(2)}) async-start(s8[14155776]{0:T(1024)(128)(4,1)} %bitcast.209), calls=%async_computation.1 | async-start | bytes 8388608
  5.8 22.9 %slice-start.2 = ((s8[14155776]{0:T(1024)(128)(4,1)}), s8[1572864]{0:T(1024)(128)(4,1)S(1)}, s32[]{:S(2)}) async-start(s8[14155776]{0:T(1024)(128)(4,1)} %bitcast.209), calls=%async_computation.2 | async-start | bytes 3145728
  20.4 8.3 %slice-start.3 = ((s8[14155776]{0:T(1024)(128)(4,1)}), s8[4194304]{0:T(1024)(128)(4,1)S(1)}, s32[]{:S(2)}) async-start(s8[14155776]{0:T(1024)(128)(4,1)} %bitcast.209), calls=%async_computation.3 | async-start | bytes 8388608
  20.4 8.3 %copy-start.1 = (f32[1,2,128,1536]{3,2,1,0:T(8,128)S(1)}, f32[1,2,128,1536]{3,2,1,0:T(8,128)}, u32[]{:S(2)}) copy-start(f32[1,2,128,1536]{3,2,1,0:T(8,128)} %copy-done) | copy-start | bytes 4718596
  22.4 37.7 %collective-permute-start.5 = (f32[2,2,576,128]{3,2,1,0:T(8,128)}, f32[2,2,576,128]{3,2,1,0:T(8,128)}, u32[]{:S(2)}, u32[]{:S(2)}) collective-permute-start(f32[2,2,576,128]{3,2,1,0:T(8,128)} %get-tuple-element.26), channel_id=1, source_target_pairs={{0,3},{1,0},{2,1},{3,2},{4,7},{5,4},{6,5},{7,6},{8,11},{9,8},{10,9... | collective-permute-start | bytes 3538952 | tf_op jit(solution)/shard_map/ppermute | solution.py:84
  27.4 80.1 %collective-permute-start.3 = (f32[2,2,576,128]{3,2,1,0:T(8,128)}, f32[2,2,576,128]{3,2,1,0:T(8,128)}, u32[]{:S(2)}, u32[]{:S(2)}) collective-permute-start(f32[2,2,576,128]{3,2,1,0:T(8,128)} %get-tuple-element.27), channel_id=1, source_target_pairs={{0,1},{1,2},{2,3},{3,0},{4,5},{5,6},{6,7},{7,4},{8,9},{9,10},{10,1... | collective-permute-start | bytes 3538952 | tf_op jit(solution)/shard_map/ppermute | solution.py:84
  27.7 103.3 %collective-permute-start.4 = (f32[2,2,576,128]{3,2,1,0:T(8,128)}, f32[2,2,576,128]{3,2,1,0:T(8,128)}, u32[]{:S(2)}, u32[]{:S(2)}) collective-permute-start(f32[2,2,576,128]{3,2,1,0:T(8,128)} %get-tuple-element.29), channel_id=1, source_target_pairs={{0,2},{1,3},{2,0},{3,1},{4,6},{5,7},{6,4},{7,5},{8,10},{9,11},{10,... | collective-permute-start | bytes 3538952 | tf_op jit(solution)/shard_map/ppermute | solution.py:84
  28.7 15.2 %slice-start.4 = ((s8[14155776]{0:T(1024)(128)(4,1)}), s8[4194304]{0:T(1024)(128)(4,1)S(1)}, s32[]{:S(2)}) async-start(s8[14155776]{0:T(1024)(128)(4,1)} %bitcast.215), calls=%async_computation.4 | async-start | bytes 8388608
  28.7 15.2 %slice-start.5 = ((s8[14155776]{0:T(1024)(128)(4,1)}), s8[4194304]{0:T(1024)(128)(4,1)S(1)}, s32[]{:S(2)}) async-start(s8[14155776]{0:T(1024)(128)(4,1)} %bitcast.215), calls=%async_computation.5 | async-start | bytes 8388608
  35.3 8.6 %slice-start.6 = ((s8[14155776]{0:T(1024)(128)(4,1)}), s8[4194304]{0:T(1024)(128)(4,1)S(1)}, s32[]{:S(2)}) async-start(s8[14155776]{0:T(1024)(128)(4,1)} %bitcast.215), calls=%async_computation.6 | async-start | bytes 8388608
  36.8 7.1 %slice-start.7 = ((s8[14155776]{0:T(1024)(128)(4,1)}), s8[1572864]{0:T(1024)(128)(4,1)S(1)}, s32[]{:S(2)}) async-start(s8[14155776]{0:T(1024)(128)(4,1)} %bitcast.215), calls=%async_computation.7 | async-start | bytes 3145728
  50.5 1.4 copy-start.5
  51.9 3.9 %copy-start.4 = (f32[1,2,576,128]{3,2,1,0:T(8,128)S(1)}, f32[1,2,576,128]{3,2,1,0:T(8,128)}, u32[]{:S(2)}) copy-start(f32[1,2,576,128]{3,2,1,0:T(8,128)} %get-tuple-element.55) | copy-start | bytes 1769476
  51.9 7.1 %copy-start.3 = (f32[1,2,576,128]{3,2,1,0:T(8,128)S(1)}, f32[1,2,576,128]{3,2,1,0:T(8,128)}, u32[]{:S(2)}) copy-start(f32[1,2,576,128]{3,2,1,0:T(8,128)} %get-tuple-element.56) | copy-start | bytes 1769476
  53.0 131.3 %collective-permute-start.2 = (f32[2,2,576,128]{3,2,1,0:T(8,128)}, f32[2,2,576,128]{3,2,1,0:T(8,128)}, u32[]{:S(2)}, u32[]{:S(2)}) collective-permute-start(f32[2,2,576,128]{3,2,1,0:T(8,128)} %pad_maximum_fusion.6), channel_id=1, source_target_pairs={{0,3},{1,0},{2,1},{3,2},{4,7},{5,4},{6,5},{7,6},{8,11},{9,8},{10,9... | collective-permute-start | bytes 3538952 | tf_op jit(solution)/shard_map/ppermute | solution.py:84
  56.9 199.4 %collective-permute-start.1 = (f32[2,2,576,128]{3,2,1,0:T(8,128)}, f32[2,2,576,128]{3,2,1,0:T(8,128)}, u32[]{:S(2)}, u32[]{:S(2)}) collective-permute-start(f32[2,2,576,128]{3,2,1,0:T(8,128)} %pad_maximum_fusion.5), channel_id=1, source_target_pairs={{0,2},{1,3},{2,0},{3,1},{4,6},{5,7},{6,4},{7,5},{8,10},{9,11},{10,... | collective-permute-start | bytes 3538952 | tf_op jit(solution)/shard_map/ppermute | solution.py:84
  60.1 196.3 %collective-permute-start = (f32[2,2,576,128]{3,2,1,0:T(8,128)}, f32[2,2,576,128]{3,2,1,0:T(8,128)}, u32[]{:S(2)}, u32[]{:S(2)}) collective-permute-start(f32[2,2,576,128]{3,2,1,0:T(8,128)} %pad_maximum_fusion.4), channel_id=1, source_target_pairs={{0,1},{1,2},{2,3},{3,0},{4,5},{5,6},{6,7},{7,4},{8,9},{9,10},{10,1... | collective-permute-start | bytes 3538952 | tf_op jit(solution)/shard_map/ppermute | solution.py:84
  104.2 152.1 %copy-start.2 = (f32[1,2,576,128]{3,2,1,0:T(8,128)S(1)}, f32[1,2,576,128]{3,2,1,0:T(8,128)}, u32[]{:S(2)}) copy-start(f32[1,2,576,128]{3,2,1,0:T(8,128)} %get-tuple-element.53) | copy-start | bytes 1769476
  131.0 161.3 %collective-permute-start.8 = (f32[1,2,576,128]{3,2,1,0:T(8,128)}, f32[1,2,576,128]{3,2,1,0:T(8,128)}, u32[]{:S(2)}, u32[]{:S(2)}) collective-permute-start(f32[1,2,576,128]{3,2,1,0:T(8,128)} %get-tuple-element.11), channel_id=1, source_target_pairs={{0,1},{1,2},{2,3},{3,0},{4,5},{5,6},{6,7},{7,4},{8,9},{9,10},{10,1... | collective-permute-start | bytes 1769480 | tf_op jit(solution)/shard_map/ppermute | solution.py:84
  180.8 111.5 %collective-permute-start.9 = (f32[1,2,576,128]{3,2,1,0:T(8,128)}, f32[1,2,576,128]{3,2,1,0:T(8,128)}, u32[]{:S(2)}, u32[]{:S(2)}) collective-permute-start(f32[1,2,576,128]{3,2,1,0:T(8,128)} %get-tuple-element.12), channel_id=1, source_target_pairs={{0,2},{1,3},{2,0},{3,1},{4,6},{5,7},{6,4},{7,5},{8,10},{9,11},{10,... | collective-permute-start | bytes 1769480 | tf_op jit(solution)/shard_map/ppermute | solution.py:84
  184.2 108.1 %collective-permute-start.10 = (f32[1,2,576,128]{3,2,1,0:T(8,128)}, f32[1,2,576,128]{3,2,1,0:T(8,128)}, u32[]{:S(2)}, u32[]{:S(2)}) collective-permute-start(f32[1,2,576,128]{3,2,1,0:T(8,128)} %get-tuple-element.13), channel_id=1, source_target_pairs={{0,3},{1,0},{2,1},{3,2},{4,7},{5,4},{6,5},{7,6},{8,11},{9,8},{10,9... | collective-permute-start | bytes 1769480 | tf_op jit(solution)/shard_map/ppermute | solution.py:84
  262.1 31.8 %collective-permute-start.7 = (f32[2,1,2,288,512]{4,3,1,2,0:T(8,128)S(1)}, f32[2,1,2,288,512]{4,3,1,2,0:T(8,128)}, u32[]{:S(2)}, u32[]{:S(2)}) collective-permute-start(f32[2,1,2,288,512]{4,3,1,2,0:T(8,128)S(1)} %get-tuple-element.24), channel_id=1, source_target_pairs={{0,4},{4,8},{8,12},{12,16},{16,20},{20,24},{24,28},{1,5},{5,9},{9,... | collective-permute-start | bytes 7077896 | tf_op jit(solution)/shard_map/ppermute | solution.py:99
  264.8 29.1 %collective-permute-start.6 = (f32[2,1,2,288,512]{4,3,1,2,0:T(8,128)S(1)}, f32[2,1,2,288,512]{4,3,1,2,0:T(8,128)}, u32[]{:S(2)}, u32[]{:S(2)}) collective-permute-start(f32[2,1,2,288,512]{4,3,1,2,0:T(8,128)S(1)} %get-tuple-element.25), channel_id=1, source_target_pairs={{4,0},{8,4},{12,8},{16,12},{20,16},{24,20},{28,24},{5,1},{9,5},{13... | collective-permute-start | bytes 7077896 | tf_op jit(solution)/shard_map/ppermute | solution.py:100
  292.3 1.6 copy-start.6
  328.8 25.4 %collective-permute-start.11 = (f32[]{:T(128)}, f32[]{:T(128)}, u32[]{:S(2)}, u32[]{:S(2)}) collective-permute-start(f32[]{:T(128)} %get-tuple-element.14), channel_id=1, source_target_pairs={{0,4},{4,8},{8,12},{12,16},{16,20},{20,24},{24,28},{28,0},{1,5},{5... | collective-permute-start | bytes 20 | tf_op jit(solution)/shard_map/ppermute | solution.py:48
  355.6 4.4 %collective-permute-start.12 = (f32[]{:T(128)}, f32[]{:T(128)}, u32[]{:S(2)}, u32[]{:S(2)}) collective-permute-start(f32[]{:T(128)} %max.15), channel_id=1, source_target_pairs={{0,8},{4,12},{8,16},{12,20},{16,24},{20,28},{24,0},{28,4},{1,9},{5... | collective-permute-start | bytes 20 | tf_op jit(solution)/shard_map/ppermute | solution.py:48
  360.8 4.5 %collective-permute-start.13 = (f32[]{:T(128)}, f32[]{:T(128)}, u32[]{:S(2)}, u32[]{:S(2)}) collective-permute-start(f32[]{:T(128)} %max.16), channel_id=1, source_target_pairs={{0,16},{4,20},{8,24},{12,28},{16,0},{20,4},{24,8},{28,12},{1,17},{... | collective-permute-start | bytes 20 | tf_op jit(solution)/shard_map/ppermute | solution.py:48
  365.9 5.3 %collective-permute-start.14 = (f32[]{:T(128)}, f32[]{:T(128)}, u32[]{:S(2)}, u32[]{:S(2)}) collective-permute-start(f32[]{:T(128)} %max.17), channel_id=1, source_target_pairs={{0,1},{1,2},{2,3},{3,0},{4,5},{5,6},{6,7},{7,4},{8,9},{9,10},{10,1... | collective-permute-start | bytes 20 | tf_op jit(solution)/shard_map/ppermute | solution.py:48
  371.9 4.5 %collective-permute-start.15 = (f32[]{:T(128)}, f32[]{:T(128)}, u32[]{:S(2)}, u32[]{:S(2)}) collective-permute-start(f32[]{:T(128)} %max.18), channel_id=1, source_target_pairs={{0,2},{1,3},{2,0},{3,1},{4,6},{5,7},{6,4},{7,5},{8,10},{9,11},{10,... | collective-permute-start | bytes 20 | tf_op jit(solution)/shard_map/ppermute | solution.py:48
